TPU v7x, 256 devices: a whole 4x4x8 slice. The times are simulated.
256 devices in a mesh: cell: 8 (over y, x_lo), gene: 32 (over z, x_hi, core).
Axes of the slice: x: 4 (x_hi: 2, x_lo: 2; x = x_hi * 2 + x_lo), y: 4, z: 8, core: 2. Of those that a mesh axis runs over, the one named last changes fastest.
Arguments:
- counts: float32 [2048, 16384], P('cell', 'gene'), as said below
- gene_mean: float32 [16384], P('gene'), may hold values from -5 to 10
- gene_std: float32 [16384], P('gene'), may hold values from 0 to 10
Outputs:
- gram: float32 [16384, 16384], P('gene', 'cell')
Inputs may be any that keep to these rules, and one draw needn't show every extreme that they name: `counts`: whole numbers; every cell has at least one count.
All inputs are finite; a program needn't handle non-finite values.
Results may differ from a plain program's by a relative error of at most 0.013.
Values may be sent and summed in bfloat16 or wider, within the bound.
A program may use at most 128 MiB of HBM per device.

v0:
```python
import jax
import jax.numpy as jnp
from jax import lax
from jax.sharding import PartitionSpec as P


def standardize(counts, library, gene_mean, gene_std):
    normal = jnp.log1p(counts / library[:, None] * 10000.0)
    spread = jnp.maximum(gene_std, 0.1)
    scaled = jnp.minimum((normal - gene_mean[None, :]) / spread[None, :], 10.0)
    return scaled.astype(jnp.bfloat16)


def shards(counts, gene_mean, gene_std):
    cell_rows = counts.shape[0]
    library = lax.psum(jnp.sum(counts, axis=1), "gene")
    mine = standardize(counts, library, gene_mean, gene_std)
    whole = lax.all_gather(mine, "gene", axis=1, tiled=True)
    groups = lax.axis_size("cell")
    total_cells = cell_rows * groups
    summed = lax.psum_scatter(
        lax.dot_general(
            whole, mine, (((0,), (0,)), ((), ())), preferred_element_type=jnp.float32
        ).astype(jnp.bfloat16),
        "cell",
        scatter_dimension=0,
        tiled=True,
    ).astype(jnp.float32)
    return summed.T / total_cells


def solution(mesh):
    placed = (P("cell", "gene"), P("gene"), P("gene"))
    return jax.shard_map(
        shards, mesh=mesh, in_specs=placed, out_specs=P("gene", "cell"), check_vma=False
    )
```

profile of v0, /device:TPU:1, one launch (start us, length us, event | category | flops | bytes accessed | tf_op | source)
XLA Modules:
  0.0 542.9 jit_solution(7759960904964985445)
XLA Ops:
  6.5 0.0 all-gather.2.cloned.1.call-start
  6.5 1.2 reduce_sum.9
  7.7 69.0 %psum.7 = f32[256]{0:T(256)S(1)} all-reduce(f32[256]{0:T(256)S(1)} %reduce_sum.9), channel_id=1, replica_groups=mesh['cell'=8,'gene'=32] {'gene'}, use_global_device_ids=true, to_apply=%region_1.0 | all-reduce | flops 256 | bytes 2048 | tf_op jit(solution)/shard_map/psum | solution.py:16
  76.7 0.7 broadcast_maximum_fusion
  77.3 2.1 minimum_convert_fusion
  79.4 0.0 all-gather.2.cloned.1.call-update
  79.4 0.0 reduce-scatter.2.cloned.1.call-start
  79.5 108.3 %all-gather.2.cloned.1.call-done = bf16[256,16384]{1,0:T(8,128)(2,1)} async-done(((bf16[256,512]{1,0:T(8,128)(2,1)}), bf16[256,16384]{1,0:T(8,128)(2,1)}) %all-gather.2.cloned.1.call-update) | async-done | bytes 8388624 | tf_op jit(solution)/shard_map/all_gather | solution.py:18
  187.8 13.7 %convolution_convert_fusion = bf16[16384,512]{1,0:T(8,128)(2,1)} fusion(bf16[256,16384]{1,0:T(8,128)(2,1)} %all-gather.2.cloned.1.call-done, bf16[256,512]{1,0:T(8,128)(2,1)} %minimum_convert_fusion), kind=kOutput, calls=%fused_computation | convolution fusion | flops 4303355904 | bytes 25427968 | tf_op jit(solution)/shard_map/dot_general | solution.py:22
  201.5 0.0 reduce-scatter.2.cloned.1.call-update
  201.5 325.1 %reduce-scatter.2.cloned.1.call-done = bf16[2048,512]{1,0:T(8,128)(2,1)} async-done(((bf16[16384,512]{1,0:T(8,128)(2,1)}), bf16[2048,512]{1,0:T(8,128)(2,1)}) %reduce-scatter.2.cloned.1.call-update) | async-done | bytes 2097168 | tf_op jit(solution)/shard_map/reduce_scatter | solution.py:21
  526.6 4.1 multiply_bitcast_fusion
  530.7 5.3 copy.4
Async XLA Ops:
  6.5 181.3 %all-gather.2.cloned.1.call-start = ((), (), s32[]{:S(2)}) async-start(), calls=%async_computation.1 | async-start | bytes 8650752 | tf_op jit(solution)/shard_map/all_gather | solution.py:18
  79.4 447.2 %reduce-scatter.2.cloned.1.call-start = ((), (), s32[]{:S(2)}) async-start(), calls=%async_computation.2 | async-start | bytes 18874368 | tf_op jit(solution)/shard_map/reduce_scatter | solution.py:21
Sparse Core Ops, SparseCore 0:
  79.6 108.1 all-gather.1
  201.6 324.9 reduce-scatter.1
where the time goes:
time: 543 us
  waiting for transfers between devices  433 us (80%)
  blocking collectives  69 us (13%)
  matrix products  13.7 us (3%)
  between operations  13.4 us (2%)
  other arithmetic  8.02 us (1%)
    reduce_scatter x1, waiting for transfers between devices, shards(): lax.psum_scatter(lax.dot_general(whole, mine, (((0,), (0,)), ((), ())), p...  325 us
    all_gather x1, waiting for transfers between devices, shards(): whole = lax.all_gather(mine, 'gene', axis=1, tiled=True)  108 us
    psum x1, blocking collectives, shards(): library = lax.psum(jnp.sum(counts, axis=1), 'gene')  69 us
    dot_general x1, matrix products, shards(): lax.dot_general(whole, mine, (((0,), (0,)), ((), ())), preferred_element_...  13.7 us
  transfers between devices with their start and end apart: 2, of which 2 were waited for; matrix products, arithmetic and copies ran while one was open for 0% of the time, Pallas kernels for 0%

commit v1 on v0

v1 whole, which is shorter than its diff:
```python
import jax
import jax.numpy as jnp
from jax import lax
from jax.experimental import pallas as pl
from jax.experimental.pallas import tpu as pltpu
from jax.sharding import PartitionSpec as P

MESH = pl.DeviceIdType.MESH
BF16, F32 = jnp.bfloat16, jnp.float32


def kernel(
    counts, mean, std, out,
    raw, part, libs, rows, both, half,
    raw_sem, lib_send, lib_recv, row_send, row_recv, share_send,
    cut_send, cut_recv, ring_send, ring_recv, swap_send, swap_recv, twin_send, twin_recv,
):
    cell, gene = lax.axis_index("cell"), lax.axis_index("gene")
    y, low = cell // 2, cell % 2
    z, high, core = gene // 4, (gene // 2) % 2, gene % 2

    def at(cell_, z_, high_, core_):
        return (cell_, z_ * 4 + high_ * 2 + core_)

    def send(src, dst, send_sem, recv_sem, device):
        return pltpu.make_async_remote_copy(
            src_ref=src,
            dst_ref=dst,
            send_sem=send_sem,
            recv_sem=recv_sem,
            device_id=device,
            device_id_type=MESH,
        )

    fetch = pltpu.make_async_copy(counts, raw, raw_sem)
    fetch.start()

    barrier = pltpu.get_barrier_semaphore()

    def greet(device):
        pl.semaphore_signal(barrier, inc=1, device_id=device, device_id_type=MESH)

    @pl.loop(1, 32)
    def _(off):
        greet((cell, (gene + off) % 32))

    own_chunk = cell == z

    @pl.loop(0, 16)
    def _(n):
        from_high, from_cell = n // 8, n % 8
        itself = own_chunk & (from_high == high) & (from_cell == cell)

        @pl.when(jnp.logical_not(itself))
        def _():
            greet(at(from_cell, cell, from_high, core))

    mirror = y * 2 + (1 - low)
    greet(at(mirror, z, high, core))
    for dy in (1, 2, 3):
        greet(at(((y + dy) % 4) * 2 + low, z, high, core))

    fetch.wait()
    sums = jnp.sum(raw[...], axis=1, keepdims=True)
    part[...] = jnp.broadcast_to(sums, (256, 128)).T[0:1, :]
    libs[gene] = part[...]

    pl.semaphore_wait(barrier, jnp.where(own_chunk, 31 + 15 + 4, 31 + 16 + 4))

    @pl.loop(1, 32)
    def _(off):
        send(
            part, libs.at[gene], lib_send.at[off], lib_recv.at[gene],
            (cell, (gene + off) % 32),
        ).start()

    @pl.loop(1, 32)
    def _(off):
        other = (gene + off) % 32
        send(part, libs.at[other], lib_send.at[off], lib_recv.at[other], (cell, other)).wait_recv()

    total = libs[0]
    for n in range(1, 32):
        total = total + libs[n]
    library = jnp.broadcast_to(total, (128, 256)).T
    library = jnp.concatenate([library] * 4, axis=1)
    normal = jnp.log1p(raw[...] / library * 10000.0)
    spread = jnp.maximum(std[...], 0.1)
    scaled = jnp.minimum((normal - mean[...]) / spread, 10.0).astype(BF16)
    rows[cell] = scaled.reshape(16, 16, 512)

    def cut(j, to_high):
        itself = own_chunk & (j == z) & (to_high == high)
        index = j * 2 + to_high
        device = at(z, j, to_high, core)
        pieces = (
            (rows.at[cell, pl.ds(2 * j, 2), :, pl.ds(0, 256)],
             both.at[core, j, high, :, cell], 0),
            (rows.at[cell, 2 * j + to_high, :, pl.ds(256, 256)],
             half.at[core, j, to_high, high, cell], 1),
        )
        copies = [
            send(src, dst, cut_send.at[n, index], cut_recv.at[n, high, cell], device)
            for src, dst, n in pieces
        ]
        local = [
            pltpu.make_async_copy(src, dst, cut_recv.at[n, high, cell])
            for src, dst, n in pieces
        ]
        return itself, copies, local

    @pl.loop(0, 16)
    def _(n):
        itself, copies, local = cut((z + 4 + n // 2) % 8, n % 2)

        @pl.when(itself)
        def _():
            for copy in local:
                copy.start()

        @pl.when(jnp.logical_not(itself))
        def _():
            for copy in copies:
                copy.start()

    beside = at(mirror, z, high, core)
    along = [((y + dy) % 4) * 2 + low for dy in (1, 3, 2)]
    across = [((y + dy) % 4) * 2 + low for dy in (3, 1, 2)]
    share = send(rows.at[cell], rows.at[cell], share_send, row_recv.at[cell], beside)
    share.start()
    own_rows = [
        send(rows.at[cell], rows.at[cell], row_send.at[0, n], row_recv.at[cell], at(c, z, high, core))
        for n, c in enumerate(along)
    ]
    for copy in own_rows:
        copy.start()

    out[...] = jnp.zeros_like(out)

    @pl.loop(0, 16)
    def _(n):
        from_high, from_cell = n // 8, n % 8
        device = at(from_cell, cell, from_high, core)
        send(
            rows.at[cell, pl.ds(0, 2), :, pl.ds(0, 256)],
            both.at[core, z, from_high, :, from_cell],
            cut_send.at[0, 0], cut_recv.at[0, from_high, from_cell], device,
        ).wait_recv()
        send(
            rows.at[cell, 0, :, pl.ds(256, 256)],
            half.at[core, z, high, from_high, from_cell],
            cut_send.at[1, 0], cut_recv.at[1, from_high, from_cell], device,
        ).wait_recv()

    ahead, behind = at(cell, (z + 1) % 8, high, core), at(cell, (z + 7) % 8, high, core)
    partner = at(cell, z, 1 - high, core)
    twin = at(cell, z, high, 1 - core)
    parts = (("half", 0), ("both", 0), ("half", 1), ("both", 1))

    def piece(kind, side, j):
        return both.at[core, j, side] if kind == "both" else half.at[core, j, high, side]

    def ring(way, hop, n):
        j = (z + 8 - hop if way == 0 else z + hop) % 8
        ref = piece(*parts[n], j)
        return send(ref, ref, ring_send.at[way, hop, n], ring_recv.at[way, hop, n], (ahead, behind)[way])

    def arrival(way, hop, n):
        j = (z + 7 - hop if way == 0 else z + 1 + hop) % 8
        ref = piece(*parts[n], j)
        return send(ref, ref, ring_send.at[way, hop, n], ring_recv.at[way, hop, n], (ahead, behind)[way])

    def place(q):
        return (z + (0, 7, 1, 6, 2, 5, 3, 4)[q]) % 8

    def swap(q, side):
        ref = half.at[core, place(q), high, side]
        return send(ref, ref, swap_send.at[q, side], swap_recv.at[q, side], partner)

    def swapped(q, side):
        ref = half.at[core, place(q), 1 - high, side]
        return send(ref, ref, swap_send.at[q, side], swap_recv.at[q, side], partner)

    def hand(q, kind):
        buf = both if kind == 0 else half
        ref = buf.at[core, place(q)]
        return send(ref, ref, twin_send.at[q, kind], twin_recv.at[q, kind], twin)

    def handed(q, kind):
        buf = both if kind == 0 else half
        ref = buf.at[1 - core, place(q)]
        return send(ref, ref, twin_send.at[q, kind], twin_recv.at[q, kind], twin)

    def finish_swap(q):
        for side in (0, 1):
            swapped(q, side).wait_recv()
        hand(q, 1).start()

    def multiply(q):
        j = place(q)
        handed(q, 0).wait_recv()
        handed(q, 1).wait_recv()
        left = jnp.concatenate(
            [rows[i, 2 * j + t] for t in (0, 1) for i in range(8)], axis=0
        ).T

        @pl.loop(0, 4)
        def _(n):
            side, other = n // 2, n % 2
            right = jnp.concatenate(
                [
                    both[other, j, side].reshape(256, 256),
                    half[other, j, :, side].reshape(256, 256),
                ],
                axis=1,
            )
            columns = pl.ds(pl.multiple_of(n * 512, 512), 512)
            out[:, columns] += jnp.dot(left, right, preferred_element_type=F32)

    for n in range(4):
        ring(0, 0, n).start()
        ring(1, 0, n).start()
        if parts[n][0] == "half":
            swap(0, parts[n][1]).start()
    hand(0, 0).start()

    row_recv_wait = lambda c: send(
        rows.at[c], rows.at[c], share_send, row_recv.at[c], beside
    ).wait_recv()
    row_recv_wait(mirror)
    far_rows = [
        send(rows.at[mirror], rows.at[mirror], row_send.at[1, n], row_recv.at[mirror], at(c, z, high, core))
        for n, c in enumerate(along)
    ]
    for copy in far_rows:
        copy.start()

    for hop in range(4):
        right_q, left_q = 2 * hop + 1, 2 * hop + 2
        for n in range(4):
            kind, side = parts[n]
            for way in (0, 1):
                q = 7 if hop == 3 else (right_q, left_q)[way]
                if hop == 3 and side != way:
                    continue
                arrival(way, hop, n).wait_recv()
                if hop < 2 or (hop == 2 and side == way):
                    ring(way, hop + 1, n).start()
                if kind == "half":
                    swap(q, side).start()
            if n == 2:
                for q in ((0,), (1, 2), (3, 4), (5, 6))[hop]:
                    finish_swap(q)
            if hop == 2:
                if n == 0:
                    for c in across:
                        row_recv_wait(c)
                    for c in across:
                        row_recv_wait(c + 1 - 2 * low)
                    multiply(0)
                if n == 1:
                    multiply(1)
                if n == 2:
                    multiply(2)
        if hop < 3:
            hand(right_q, 0).start()
            hand(left_q, 0).start()
        else:
            hand(7, 0).start()
    multiply(3)
    multiply(4)
    finish_swap(7)
    multiply(5)
    multiply(6)
    multiply(7)

    @pl.loop(1, 32)
    def _(off):
        send(part, libs.at[gene], lib_send.at[off], lib_recv.at[gene], (cell, (gene + off) % 32)).wait_send()

    @pl.loop(0, 16)
    def _(n):
        itself, copies, _ = cut((z + 4 + n // 2) % 8, n % 2)

        @pl.when(jnp.logical_not(itself))
        def _():
            for copy in copies:
                copy.wait_send()

    share.wait_send()
    for copy in own_rows + far_rows:
        copy.wait_send()
    for way in (0, 1):
        for hop in range(4):
            for n in range(4):
                if hop < 3 or parts[n][1] == way:
                    ring(way, hop, n).wait_send()
    for q in range(8):
        for side in (0, 1):
            swap(q, side).wait_send()
            hand(q, side).wait_send()


def shards(counts, gene_mean, gene_std):
    dma = pltpu.SemaphoreType.DMA
    gram = pl.pallas_call(
        kernel,
        out_shape=jax.ShapeDtypeStruct((512, 2048), F32),
        in_specs=[
            pl.BlockSpec(memory_space=pl.ANY),
            pl.BlockSpec(memory_space=pltpu.VMEM),
            pl.BlockSpec(memory_space=pltpu.VMEM),
        ],
        out_specs=pl.BlockSpec(memory_space=pltpu.VMEM),
        scratch_shapes=[
            pltpu.VMEM((256, 512), F32),
            pltpu.VMEM((1, 256), F32),
            pltpu.VMEM((32, 1, 256), F32),
            pltpu.VMEM((8, 16, 16, 512), BF16),
            pltpu.VMEM((2, 8, 2, 2, 8, 16, 256), BF16),
            pltpu.VMEM((2, 8, 2, 2, 8, 16, 256), BF16),
            dma,
            dma((32,)),
            dma((32,)),
            dma((2, 3)),
            dma((8,)),
            dma,
            dma((2, 16)),
            dma((2, 2, 8)),
            dma((2, 4, 4)),
            dma((2, 4, 4)),
            dma((8, 2)),
            dma((8, 2)),
            dma((8, 2)),
            dma((8, 2)),
        ],
        compiler_params=pltpu.CompilerParams(
            collective_id=0, has_side_effects=True, vmem_limit_bytes=40 << 20
        ),
        cost_estimate=pl.CostEstimate(
            flops=2 * 512 * 2048 * 2048, bytes_accessed=5 << 20, transcendentals=1 << 17
        ),
    )(counts, gene_mean.reshape(1, 512), gene_std.reshape(1, 512))
    return gram * (1.0 / 2048)


def solution(mesh):
    placed = (P("cell", "gene"), P("gene"), P("gene"))
    return jax.shard_map(
        shards, mesh=mesh, in_specs=placed, out_specs=P("gene", "cell"), check_vma=False
    )
```

time: 543 us -> 80.6 us (0.15)
  waiting for transfers between devices: 433 us -> 0 us
  Pallas kernels: 0 us -> 75.7 us
  blocking collectives: 69 us -> 0 us
  matrix products: 13.7 us -> 0 us
  between operations: 13.4 us -> 0.01 us
  other arithmetic: 8.02 us -> 2.34 us
    reduce_scatter x1 -> x0, waiting for transfers between devices: 325 us -> none  [shards(): lax.psum_scatter(lax.dot_general(whole, mine, (((0,), (0,)), ((), ())), p...]
    all_gather x1 -> x0, waiting for transfers between devices: 108 us -> none  [shards(): whole = lax.all_gather(mine, 'gene', axis=1, tiled=True)]
    pallas_call x0 -> x1, Pallas kernels: none -> 75.7 us  [shards(): pl.pallas_call(kernel, out_shape=jax.ShapeDtypeStruct((512, 2048), F32),...]
    psum x1 -> x0, blocking collectives: 69 us -> none  [shards(): library = lax.psum(jnp.sum(counts, axis=1), 'gene')]
    dot_general x1 -> x0, matrix products: 13.7 us -> none  [shards(): lax.dot_general(whole, mine, (((0,), (0,)), ((), ())), preferred_element_...]
  transfers between devices with their start and end apart: 2 -> 0, of which waited for: 2 -> 0; matrix products, arithmetic and copies ran while one was open for 0% -> 0% of each run, Pallas kernels for 0% -> 0%
where the time goes in v1:
time: 80.6 us; the launch traced here: 80.5 us
  Pallas kernels  75.7 us (94%)
  local copies, waits for them, and re-layouts  2.4 us (3%)
  other arithmetic  2.34 us (3%)
    pallas_call x1, Pallas kernels, shards(): pl.pallas_call(kernel, out_shape=jax.ShapeDtypeStruct((512, 2048), F32),...  75.7 us
    unnamed x6, local copies, waits for them, and re-layouts  2.4 us
    mul x1, other arithmetic, shards(): return gram * (1.0 / 2048)  2.34 us

profile of v1, /device:TPU:1, one launch (start us, length us, event | category | flops | bytes accessed | tf_op | source)
XLA Modules:
  0.0 80.5 jit_solution(6069553592589047376)
XLA Ops:
  0.0 0.0 copy-start
  0.0 1.0 %copy-done = f32[256,512]{1,0:T(8,128)S(1)} copy-done((f32[256,512]{1,0:T(8,128)S(1)}, f32[256,512]{1,0:T(8,128)}, u32[]{:S(2)}) %copy-start) | copy-done | bytes 524312
  1.0 0.0 copy-start.1
  1.0 0.7 copy-done.1
  1.7 0.0 copy-start.2
  1.7 0.7 copy-done.2
  2.4 75.7 %shard_map.37 = f32[512,2048]{1,0:T(8,128)S(1)} custom-call(f32[256,512]{1,0:T(8,128)S(1)} %copy-done, f32[1,512]{1,0:T(1,128)S(1)} %bitcast.2, f32[1,512]{1,0:T(1,128)S(1)} %bitcast.3), custom_call_target="tpu_custom_call" | custom-call | flops 4294967296 | bytes 5242880 | tf_op jit(solution)/shard_map/pallas_call | solution.py:306
  78.1 2.3 %broadcast_multiply_fusion = f32[512,2048]{1,0:T(8,128)} fusion(f32[512,2048]{1,0:T(8,128)S(1)} %shard_map.37), kind=kLoop, calls=%fused_computation | loop fusion | flops 1048576 | bytes 8388608 | tf_op jit(solution)/shard_map/mul | solution.py:344
Async XLA Ops:
  0.0 1.0 %copy-start = (f32[256,512]{1,0:T(8,128)S(1)}, f32[256,512]{1,0:T(8,128)}, u32[]{:S(2)}) copy-start(f32[256,512]{1,0:T(8,128)} %counts.1) | copy-start | bytes 1572868
  1.0 0.7 copy-start.1
  1.7 0.7 copy-start.2

commit v2 on v0

v2 whole, which is shorter than its diff:
```python
import jax
import jax.numpy as jnp
from jax import lax
from jax.experimental import pallas as pl
from jax.experimental.pallas import tpu as pltpu
from jax.sharding import PartitionSpec as P

MESH = pl.DeviceIdType.MESH
BF16, F32 = jnp.bfloat16, jnp.float32
SHARED = (256, 256)
PLACES = (0, 7, 1, 6, 2, 5, 3, 4)


def kernel(
    counts, mean, std, out,
    raw, centre, width, part, libs, rows, cols, lhs,
    raw_sem, lib_send, lib_recv, row_send, row_recv, cut_send, cut_recv,
    ring_send, ring_recv, swap_send, swap_recv, twin_send, twin_recv,
):
    cell, gene = lax.axis_index("cell"), lax.axis_index("gene")
    y, low = cell // 2, cell % 2
    z, high, core = gene // 4, (gene // 2) % 2, gene % 2
    other = 1 - high

    def at(cell_, z_, high_, core_):
        return (cell_, z_ * 4 + high_ * 2 + core_)

    def send(src, dst, send_sem, recv_sem, device):
        return pltpu.make_async_remote_copy(
            src_ref=src,
            dst_ref=dst,
            send_sem=send_sem,
            recv_sem=recv_sem,
            device_id=device,
            device_id_type=MESH,
        )

    ahead, behind = at(cell, (z + 1) % 8, high, core), at(cell, (z + 7) % 8, high, core)
    partner, twin = at(cell, z, other, core), at(cell, z, high, 1 - core)
    mirror = y * 2 + (1 - low)
    own_plane = cell == z

    fetches = [
        pltpu.make_async_copy(counts, raw, raw_sem.at[0]),
        pltpu.make_async_copy(mean, centre, raw_sem.at[1]),
        pltpu.make_async_copy(std, width, raw_sem.at[2]),
    ]
    for fetch in fetches:
        fetch.start()

    barrier = pltpu.get_barrier_semaphore()

    def greet(device):
        pl.semaphore_signal(barrier, inc=1, device_id=device, device_id_type=MESH)

    @pl.loop(0, 8)
    def _(n):
        @pl.when(jnp.logical_not(own_plane & (n == cell)))
        def _():
            greet(at(n, cell, high, core))

    def far_first(n):
        return 16 + ((n + 1) // 2) * (1 - 2 * (n % 2))

    @pl.loop(0, 31)
    def _(n):
        greet((cell, (gene + far_first(n)) % 32))

    greet(at(mirror, z, high, core))
    for dy in (1, 2, 3):
        greet(at(((y + dy) % 4) * 2 + low, z, high, core))

    for fetch in fetches:
        fetch.wait()
    sums = jnp.sum(raw[...], axis=1, keepdims=True)
    part[...] = jnp.broadcast_to(sums, (256, 128)).T[0:1, :]
    libs[gene] = part[...]

    pl.semaphore_wait(barrier, jnp.where(own_plane, 7 + 31 + 4, 8 + 31 + 4))

    def total_to(off):
        to = (gene + off) % 32
        return send(part, libs.at[gene], lib_send.at[off], lib_recv.at[gene], (cell, to))

    def total_from(off):
        of = (gene + off) % 32
        return send(part, libs.at[of], lib_send.at[off], lib_recv.at[of], (cell, of))

    @pl.loop(0, 31)
    def _(n):
        total_to(far_first(n)).start()

    @pl.loop(1, 32)
    def _(off):
        total_from(off).wait_recv()

    total = libs[0]
    for n in range(1, 32):
        total = total + libs[n]
    def lanes(kind, side):
        shared = SHARED[side]
        return pl.ds(shared, 512 - shared) if kind == 0 else pl.ds(0, shared)

    def cut(j, kind, side):
        return send(
            rows.at[cell, j, :, lanes(kind, side)],
            cols.at[core, j, high, cell, :, lanes(kind, side)],
            cut_send.at[kind, j],
            cut_recv.at[kind, cell],
            at(z, j, high, core),
        )

    def cut_local(j, kind, side):
        return pltpu.make_async_copy(
            rows.at[cell, j, :, lanes(kind, side)],
            cols.at[core, j, high, cell, :, lanes(kind, side)],
            cut_recv.at[kind, cell],
        )

    def cut_from(i, kind, side):
        return send(
            rows.at[cell, z, :, lanes(kind, side)],
            cols.at[core, z, high, i, :, lanes(kind, side)],
            cut_send.at[kind, z],
            cut_recv.at[kind, i],
            at(i, cell, high, core),
        )

    def cut_all(kind, side, local, remote):
        @pl.loop(0, 8)
        def _(n):
            j = (z + 4 + n) % 8
            itself = own_plane & (j == z)
            if local:

                @pl.when(itself)
                def _():
                    cut_local(j, kind, side).start()

            @pl.when(jnp.logical_not(itself))
            def _():
                remote(cut(j, kind, side))

    def on_side(side):
        return (cell // 4) == side

    factor = jnp.broadcast_to(10000.0 / total, (128, 256)).T
    inverse = 1.0 / jnp.maximum(width[...], 0.1)

    def standardize(first, last):
        factors = jnp.concatenate([factor] * ((last - first) // 128), axis=1)
        normal = jnp.log1p(raw[:, first:last] * factors)
        scaled = jnp.minimum((normal - centre[:, first:last]) * inverse[:, first:last], 10.0)
        rows[cell, :, :, first:last] = scaled.astype(BF16).reshape(8, 32, last - first)

    split = min(SHARED)
    for kind in (0, 1):
        if kind == 0:
            standardize(split, 512)
        else:
            standardize(0, split)
        if SHARED[0] == SHARED[1]:
            cut_all(kind, 0, True, lambda copy: copy.start())
        else:
            for side in (0, 1):

                @pl.when(on_side(side))
                def _():
                    cut_all(kind, side, True, lambda copy: copy.start())

    along = [((y + dy) % 4) * 2 + low for dy in (1, 3, 2)]

    def row_to(n, whose, target):
        return send(
            rows.at[whose], rows.at[whose], row_send.at[n], row_recv.at[whose],
            at(target, z, high, core),
        )

    row_copies = [row_to(0, cell, mirror)] + [
        row_to(1 + n, cell, c) for n, c in enumerate(along)
    ]
    for copy in row_copies:
        copy.start()

    out[...] = jnp.zeros_like(out)

    parts = [(s, k, side) for s, k in ((0, 0), (0, 1), (1, 1)) for side in (0, 1)]

    def place(q):
        return (z + PLACES[q]) % 8

    def view(j, whose, kind, side):
        return cols.at[core, j, whose, pl.ds(4 * side, 4), :, lanes(kind, side)]

    def piece(n, j):
        s, kind, side = parts[n]
        return view(j, other if s else high, kind, side)

    def ring(way, hop, n, j):
        ref = piece(n, j)
        return send(
            ref, ref, ring_send.at[way, hop, n], ring_recv.at[way, hop, n],
            (ahead, behind)[way],
        )

    def onward(way, hop, n):
        return ring(way, hop, n, (z + 8 - hop if way == 0 else z + hop) % 8)

    def arrival(way, hop, n):
        return ring(way, hop, n, (z + 7 - hop if way == 0 else z + 1 + hop) % 8)

    def swap(q, kind, side):
        ref = view(place(q), high, kind, side)
        return send(ref, ref, swap_send.at[kind, q, side], swap_recv.at[kind, q, side], partner)

    def swapped(q, kind, side):
        ref = view(place(q), other, kind, side)
        return send(ref, ref, swap_send.at[kind, q, side], swap_recv.at[kind, q, side], partner)

    def hand(q, s):
        ref = cols.at[core, place(q), other if s else high]
        return send(ref, ref, twin_send.at[q, s], twin_recv.at[q, s], twin)

    def handed(q, s):
        ref = cols.at[1 - core, place(q), other if s else high]
        return send(ref, ref, twin_send.at[q, s], twin_recv.at[q, s], twin)

    def finish(q):
        for side in (0, 1):
            swapped(q, 0, side).wait_recv()
        hand(q, 1).start()

    def prepare(q):
        j = place(q)
        lhs[...] = jnp.concatenate([rows[i, j] for i in range(8)], axis=0).T

    def product(q, s, own):
        j, whose, which = place(q), other if s else high, core if own else 1 - core
        right = cols[which, j, whose].reshape(256, 512)
        columns = pl.ds(pl.multiple_of((whose * 2 + which) * 512, 512), 512)
        out[:, columns] += jnp.dot(lhs[...], right, preferred_element_type=F32)

    def multiply(q):
        handed(q, 0).wait_recv()
        handed(q, 1).wait_recv()
        prepare(q)
        j = place(q)

        @pl.loop(0, 4)
        def _(n):
            right = cols[n % 2, j, n // 2].reshape(256, 512)
            columns = pl.ds(pl.multiple_of(n * 512, 512), 512)
            out[:, columns] += jnp.dot(lhs[...], right, preferred_element_type=F32)

    for kind in (0, 1):
        for side in (0, 1):
            for i in range(4 * side, 4 * side + 4):
                cut_from(i, kind, side).wait_recv()
            for way in (0, 1):
                onward(way, 0, 2 * kind + side).start()
            swap(0, kind, side).start()
    hand(0, 0).start()
    row_to(0, mirror, mirror).wait_recv()
    far_copies = [row_to(4 + n, mirror, c) for n, c in enumerate(along)]
    for copy in far_copies:
        copy.start()
    for side in (0, 1):
        swapped(0, 1, side).wait_recv()
        for way in (0, 1):
            onward(way, 0, 4 + side).start()
    finish(0)

    @pl.loop(1, 32)
    def _(off):
        total_to(off).wait_send()

    def rows_arrive():
        for dy in (1, 2, 3):
            for l in (0, 1):
                c = ((y + dy) % 4) * 2 + l
                row_to(0, c, mirror).wait_recv()

    def cuts_left():
        for kind in (0, 1):
            if SHARED[0] == SHARED[1]:
                cut_all(kind, 0, False, lambda copy: copy.wait_send())
            else:
                for side in (0, 1):

                    @pl.when(on_side(side))
                    def _():
                        cut_all(kind, side, False, lambda copy: copy.wait_send())

    def rows_left():
        for copy in row_copies + far_copies:
            copy.wait_send()

    def ring_left(hop):
        for way in (0, 1):
            for n in range(6):
                if hop < 3 or parts[n][2] == way:
                    onward(way, hop, n).wait_send()

    def swaps_left(q):
        for side in (0, 1):
            swap(q, 0, side).wait_send()
            hand(q, side).wait_send()

    beside = {
        (0, 3): [cuts_left],
        (1, 1): [lambda: finish(1)],
        (1, 3): [lambda: finish(2)],
        (1, 5): [lambda: ring_left(0)],
        (2, 0): [rows_arrive, lambda: multiply(0)],
        (2, 1): [lambda: multiply(1), lambda: finish(3)],
        (2, 2): [lambda: multiply(2), lambda: finish(4)],
        (2, 3): [rows_left, lambda: ring_left(1)],
        (2, 4): [lambda: multiply(3)],
        (2, 5): [lambda: multiply(4)],
        (3, 1): [lambda: finish(5), lambda: finish(6)],
        (3, 3): [lambda: multiply(5), lambda: multiply(6), lambda: ring_left(2), lambda: prepare(7)],
    }
    for hop in range(4):
        for n in range(6):
            s, kind, side = parts[n]
            for way in (0, 1):
                if hop == 3 and side != way:
                    continue
                arrival(way, hop, n).wait_recv()
                if hop < 2 or (hop == 2 and side == way):
                    onward(way, hop + 1, n).start()
                q = 7 if hop == 3 else 2 * hop + 1 + way
                if (s, kind) == (0, 0):
                    swap(q, 0, side).start()
                if n == 3 and hop < 3:
                    hand(q, 0).start()
            if n == 3 and hop == 3:
                hand(7, 0).start()
            for action in beside.get((hop, n), ()):
                action()
    product(7, 0, True)
    handed(7, 0).wait_recv()
    finish(7)
    product(7, 0, False)
    product(7, 1, True)
    handed(7, 1).wait_recv()
    product(7, 1, False)

    for side in (0, 1):
        swap(0, 1, side).wait_send()
    for q in range(8):
        swaps_left(q)
    ring_left(3)


def shards(counts, gene_mean, gene_std):
    dma = pltpu.SemaphoreType.DMA
    operands = counts, gene_mean.reshape(1, 512), gene_std.reshape(1, 512)
    operands = [pltpu.with_memory_space_constraint(a, pltpu.HBM) for a in operands]
    gram = pl.pallas_call(
        kernel,
        out_shape=jax.ShapeDtypeStruct((512, 2048), F32),
        in_specs=[pl.BlockSpec(memory_space=pltpu.HBM)] * 3,
        out_specs=pl.BlockSpec(memory_space=pltpu.VMEM),
        scratch_shapes=[
            pltpu.VMEM((256, 512), F32),
            pltpu.VMEM((1, 512), F32),
            pltpu.VMEM((1, 512), F32),
            pltpu.VMEM((1, 256), F32),
            pltpu.VMEM((32, 1, 256), F32),
            pltpu.VMEM((8, 8, 32, 512), BF16),
            pltpu.VMEM((2, 8, 2, 8, 32, 512), BF16),
            pltpu.VMEM((512, 256), BF16),
            dma((3,)),
            dma((32,)),
            dma((32,)),
            dma((7,)),
            dma((8,)),
            dma((2, 8)),
            dma((2, 8)),
            dma((2, 4, 6)),
            dma((2, 4, 6)),
            dma((2, 8, 2)),
            dma((2, 8, 2)),
            dma((8, 2)),
            dma((8, 2)),
        ],
        compiler_params=pltpu.CompilerParams(
            collective_id=0, has_side_effects=True, vmem_limit_bytes=40 << 20
        ),
        cost_estimate=pl.CostEstimate(
            flops=2 * 512 * 2048 * 2048, bytes_accessed=5 << 20, transcendentals=1 << 17
        ),
    )(*operands)
    return gram * (1.0 / 2048)


def solution(mesh):
    placed = (P("cell", "gene"), P("gene"), P("gene"))
    return jax.shard_map(
        shards, mesh=mesh, in_specs=placed, out_specs=P("gene", "cell"), check_vma=False
    )
```

time: 543 us -> 69.2 us (0.13)
  waiting for transfers between devices: 433 us -> 0 us
  blocking collectives: 69 us -> 0 us
  Pallas kernels: 0 us -> 66.5 us
  matrix products: 13.7 us -> 0 us
  between operations: 13.4 us -> 0.01 us
  other arithmetic: 8.02 us -> 2.59 us
    reduce_scatter x1 -> x0, waiting for transfers between devices: 325 us -> none  [shards(): lax.psum_scatter(lax.dot_general(whole, mine, (((0,), (0,)), ((), ())), p...]
    all_gather x1 -> x0, waiting for transfers between devices: 108 us -> none  [shards(): whole = lax.all_gather(mine, 'gene', axis=1, tiled=True)]
    psum x1 -> x0, blocking collectives: 69 us -> none  [shards(): library = lax.psum(jnp.sum(counts, axis=1), 'gene')]
    pallas_call x0 -> x1, Pallas kernels: none -> 66.5 us  [shards(): pl.pallas_call(kernel, out_shape=jax.ShapeDtypeStruct((512, 2048), F32),...]
    dot_general x1 -> x0, matrix products: 13.7 us -> none  [shards(): lax.dot_general(whole, mine, (((0,), (0,)), ((), ())), preferred_element_...]
  transfers between devices with their start and end apart: 2 -> 0, of which waited for: 2 -> 0; matrix products, arithmetic and copies ran while one was open for 0% -> 0% of each run, Pallas kernels for 0% -> 0%
where the time goes in v2:
time: 69.2 us; the launch traced here: 69.1 us
  Pallas kernels  66.5 us (96%)
  other arithmetic  2.59 us (4%)
    pallas_call x1, Pallas kernels, shards(): pl.pallas_call(kernel, out_shape=jax.ShapeDtypeStruct((512, 2048), F32),...  66.5 us
    mul x1, other arithmetic, shards(): return gram * (1.0 / 2048)  2.59 us

profile of v2, /device:TPU:1, one launch (start us, length us, event | category | flops | bytes accessed | tf_op | source)
XLA Modules:
  0.0 69.1 jit_solution(14568586699205762585)
XLA Ops:
  0.0 66.5 %shard_map.37 = f32[512,2048]{1,0:T(8,128)S(1)} custom-call(f32[256,512]{1,0:T(8,128)} %counts.1, f32[1,512]{1,0:T(1,128)} %bitcast.2, f32[1,512]{1,0:T(1,128)} %bitcast.3), custom_call_target="tpu_custom_call" | custom-call | flops 4294967296 | bytes 5242880 | tf_op jit(solution)/shard_map/pallas_call | solution.py:360
  66.5 2.6 %broadcast_multiply_fusion = f32[512,2048]{1,0:T(8,128)} fusion(f32[512,2048]{1,0:T(8,128)S(1)} %shard_map.37), kind=kLoop, calls=%fused_computation | loop fusion | flops 1048576 | bytes 8388608 | tf_op jit(solution)/shard_map/mul | solution.py:395

commit v3 on v2

--- a/solution.py
+++ b/solution.py
@@ -15,7 +15,7 @@
     counts, mean, std, out,
     raw, centre, width, part, libs, rows, cols, lhs,
     raw_sem, lib_send, lib_recv, row_send, row_recv, cut_send, cut_recv,
-    ring_send, ring_recv, swap_send, swap_recv, twin_send, twin_recv,
+    ring_send, ring_recv, swap_send, swap_recv, twin_send, twin_recv, last_send, last_recv,
 ):
     cell, gene = lax.axis_index("cell"), lax.axis_index("gene")
     y, low = cell // 2, cell % 2
@@ -225,32 +225,46 @@
         ref = cols.at[1 - core, place(q), other if s else high]
         return send(ref, ref, twin_send.at[q, s], twin_recv.at[q, s], twin)
 
+    def last_hand(kind, side):
+        ref = view(place(7), other, kind, side)
+        return send(ref, ref, last_send.at[kind, side], last_recv.at[kind, side], twin)
+
+    def last_handed(kind, side):
+        ref = cols.at[1 - core, place(7), other, pl.ds(4 * side, 4), :, lanes(kind, side)]
+        return send(ref, ref, last_send.at[kind, side], last_recv.at[kind, side], twin)
+
     def finish(q):
         for side in (0, 1):
             swapped(q, 0, side).wait_recv()
         hand(q, 1).start()
 
-    def prepare(q):
-        j = place(q)
-        lhs[...] = jnp.concatenate([rows[i, j] for i in range(8)], axis=0).T
-
-    def product(q, s, own):
+    def prepare(*qs):
+        for q in qs:
+            j = place(q)
+            lhs[q] = jnp.concatenate([rows[i, j] for i in range(8)], axis=0).T
+
+    def product(q, s, own, first=0, last=512):
         j, whose, which = place(q), other if s else high, core if own else 1 - core
-        right = cols[which, j, whose].reshape(256, 512)
-        columns = pl.ds(pl.multiple_of((whose * 2 + which) * 512, 512), 512)
-        out[:, columns] += jnp.dot(lhs[...], right, preferred_element_type=F32)
-
-    def multiply(q):
-        handed(q, 0).wait_recv()
-        handed(q, 1).wait_recv()
-        prepare(q)
-        j = place(q)
-
-        @pl.loop(0, 4)
-        def _(n):
-            right = cols[n % 2, j, n // 2].reshape(256, 512)
-            columns = pl.ds(pl.multiple_of(n * 512, 512), 512)
-            out[:, columns] += jnp.dot(lhs[...], right, preferred_element_type=F32)
+        right = cols[which, j, whose, :, :, first:last].reshape(256, last - first)
+        start = pl.multiple_of((whose * 2 + which) * 512 + first, 128)
+        columns = pl.ds(start, last - first)
+        out[:, columns] += jnp.dot(lhs[q], right, preferred_element_type=F32)
+
+    def multiply(s, *qs):
+        for q in qs:
+            handed(q, s).wait_recv()
+        whose = other if s else high
+
+        @pl.loop(0, 2)
+        def _(which):
+            columns = pl.ds(pl.multiple_of((whose * 2 + which) * 512, 512), 512)
+            right = [cols[which, place(q), whose].reshape(256, 512) for q in qs]
+            left = [lhs[q] for q in qs]
+            if len(qs) > 1:
+                left, right = jnp.concatenate(left, axis=1), jnp.concatenate(right, axis=0)
+            else:
+                left, right = left[0], right[0]
+            out[:, columns] += jnp.dot(left, right, preferred_element_type=F32)
 
     for kind in (0, 1):
         for side in (0, 1):
@@ -264,15 +278,18 @@
     far_copies = [row_to(4 + n, mirror, c) for n, c in enumerate(along)]
     for copy in far_copies:
         copy.start()
-    for side in (0, 1):
-        swapped(0, 1, side).wait_recv()
-        for way in (0, 1):
-            onward(way, 0, 4 + side).start()
-    finish(0)
-
-    @pl.loop(1, 32)
-    def _(off):
-        total_to(off).wait_send()
+
+    def begin_shared():
+        for side in (0, 1):
+            swapped(0, 1, side).wait_recv()
+            for way in (0, 1):
+                onward(way, 0, 4 + side).start()
+        finish(0)
+
+    def totals_left():
+        @pl.loop(1, 32)
+        def _(off):
+            total_to(off).wait_send()
 
     def rows_arrive():
         for dy in (1, 2, 3):
@@ -304,53 +321,70 @@
     def swaps_left(q):
         for side in (0, 1):
             swap(q, 0, side).wait_send()
-            hand(q, side).wait_send()
-
+        hand(q, 0).wait_send()
+        if q < 7:
+            hand(q, 1).wait_send()
+
+    def last_swapped():
+        for side in (0, 1):
+            swapped(7, 0, side).wait_recv()
+            last_hand(0, side).start()
+        product(7, 0, True)
+        product(7, 1, True, wide, 512)
+
+    wide = max(SHARED)
     beside = {
-        (0, 3): [cuts_left],
-        (1, 1): [lambda: finish(1)],
-        (1, 3): [lambda: finish(2)],
-        (1, 5): [lambda: ring_left(0)],
-        (2, 0): [rows_arrive, lambda: multiply(0)],
-        (2, 1): [lambda: multiply(1), lambda: finish(3)],
-        (2, 2): [lambda: multiply(2), lambda: finish(4)],
-        (2, 3): [rows_left, lambda: ring_left(1)],
-        (2, 4): [lambda: multiply(3)],
-        (2, 5): [lambda: multiply(4)],
-        (3, 1): [lambda: finish(5), lambda: finish(6)],
-        (3, 3): [lambda: multiply(5), lambda: multiply(6), lambda: ring_left(2), lambda: prepare(7)],
+        (0, 0): [begin_shared],
+        (1, 0): [cuts_left],
+        (2, 0): [lambda: finish(1), lambda: finish(2)],
+        (1, 1): [totals_left],
+        (2, 1): [lambda: finish(3), lambda: finish(4), rows_arrive, lambda: prepare(0, 1, 2), lambda: multiply(0, 0, 1, 2)],
+        (1, 2): [lambda: multiply(1, 0, 1, 2), lambda: prepare(3, 4)],
+        (0, 3): [lambda: multiply(0, 3, 4), lambda: multiply(1, 3, 4), lambda: prepare(5, 6, 7)],
+        (2, 2): [lambda: finish(5), lambda: finish(6), lambda: multiply(0, 5, 6), lambda: ring_left(0), rows_left],
+        (1, 3): [lambda: multiply(1, 5, 6), last_swapped],
     }
-    for hop in range(4):
-        for n in range(6):
-            s, kind, side = parts[n]
+    order = (
+        (0, 0), (1, 0), (0, 1), (2, 0), (1, 1), (0, 2),
+        (2, 1), (1, 2), (0, 3), (2, 2), (1, 3), (2, 3),
+    )
+    for p, hop in order:
+        for side in (0, 1):
+            n = 2 * p + side
             for way in (0, 1):
                 if hop == 3 and side != way:
                     continue
                 arrival(way, hop, n).wait_recv()
                 if hop < 2 or (hop == 2 and side == way):
                     onward(way, hop + 1, n).start()
-                q = 7 if hop == 3 else 2 * hop + 1 + way
-                if (s, kind) == (0, 0):
-                    swap(q, 0, side).start()
-                if n == 3 and hop < 3:
-                    hand(q, 0).start()
-            if n == 3 and hop == 3:
-                hand(7, 0).start()
-            for action in beside.get((hop, n), ()):
-                action()
-    product(7, 0, True)
+                if p == 0:
+                    swap(7 if hop == 3 else 2 * hop + 1 + way, 0, side).start()
+                if (p, hop) == (2, 3):
+                    last_hand(1, side).start()
+        if p == 1:
+            for q in (7,) if hop == 3 else (2 * hop + 1, 2 * hop + 2):
+                hand(q, 0).start()
+        for action in beside.get((p, hop), ()):
+            action()
+    product(7, 1, True, 0, wide)
     handed(7, 0).wait_recv()
-    finish(7)
     product(7, 0, False)
-    product(7, 1, True)
-    handed(7, 1).wait_recv()
-    product(7, 1, False)
-
+    for side in (0, 1):
+        last_handed(0, side).wait_recv()
+    product(7, 1, False, wide, 512)
+    for side in (0, 1):
+        last_handed(1, side).wait_recv()
+    product(7, 1, False, 0, wide)
+
+    for kind in (0, 1):
+        for side in (0, 1):
+            last_hand(kind, side).wait_send()
     for side in (0, 1):
         swap(0, 1, side).wait_send()
     for q in range(8):
         swaps_left(q)
-    ring_left(3)
+    for hop in (1, 2, 3):
+        ring_left(hop)
 
 
 def shards(counts, gene_mean, gene_std):
@@ -370,7 +404,7 @@
             pltpu.VMEM((32, 1, 256), F32),
             pltpu.VMEM((8, 8, 32, 512), BF16),
             pltpu.VMEM((2, 8, 2, 8, 32, 512), BF16),
-            pltpu.VMEM((512, 256), BF16),
+            pltpu.VMEM((8, 512, 256), BF16),
             dma((3,)),
             dma((32,)),
             dma((32,)),
@@ -384,6 +418,8 @@
             dma((2, 8, 2)),
             dma((8, 2)),
             dma((8, 2)),
+            dma((2, 2)),
+            dma((2, 2)),
         ],
         compiler_params=pltpu.CompilerParams(
             collective_id=0, has_side_effects=True, vmem_limit_bytes=40 << 20

time: 69.2 us -> 64.4 us (0.931)
  Pallas kernels: 66.5 us -> 61.7 us
    pallas_call x1, Pallas kernels: 66.5 us -> 61.7 us  [shards(): pl.pallas_call(kernel, out_shape=jax.ShapeDtypeStruct((512, 2048), F32),...]
where the time goes in v3:
time: 64.4 us; the launch traced here: 64.3 us
  Pallas kernels  61.7 us (96%)
  other arithmetic  2.59 us (4%)
    pallas_call x1, Pallas kernels, shards(): pl.pallas_call(kernel, out_shape=jax.ShapeDtypeStruct((512, 2048), F32),...  61.7 us
    mul x1, other arithmetic, shards(): return gram * (1.0 / 2048)  2.59 us

profile of v3, /device:TPU:1, one launch (start us, length us, event | category | flops | bytes accessed | tf_op | source)
XLA Modules:
  0.0 64.3 jit_solution(15543741957407530780)
XLA Ops:
  0.0 61.7 %shard_map.37 = f32[512,2048]{1,0:T(8,128)S(1)} custom-call(f32[256,512]{1,0:T(8,128)} %counts.1, f32[1,512]{1,0:T(1,128)} %bitcast.2, f32[1,512]{1,0:T(1,128)} %bitcast.3), custom_call_target="tpu_custom_call" | custom-call | flops 4294967296 | bytes 5242880 | tf_op jit(solution)/shard_map/pallas_call | solution.py:394
  61.7 2.6 %broadcast_multiply_fusion = f32[512,2048]{1,0:T(8,128)} fusion(f32[512,2048]{1,0:T(8,128)S(1)} %shard_map.37), kind=kLoop, calls=%fused_computation | loop fusion | flops 1048576 | bytes 8388608 | tf_op jit(solution)/shard_map/mul | solution.py:431

commit v4 on v3

--- a/solution.py
+++ b/solution.py
@@ -334,8 +334,8 @@
 
     wide = max(SHARED)
     beside = {
-        (0, 0): [begin_shared],
-        (1, 0): [cuts_left],
+        (0, 0): [],
+        (1, 0): [begin_shared, cuts_left],
         (2, 0): [lambda: finish(1), lambda: finish(2)],
         (1, 1): [totals_left],
         (2, 1): [lambda: finish(3), lambda: finish(4), rows_arrive, lambda: prepare(0, 1, 2), lambda: multiply(0, 0, 1, 2)],

time: 64.4 us -> 63.6 us (0.988)
  Pallas kernels: 61.7 us -> 61 us
    pallas_call x1, Pallas kernels: 61.7 us -> 61 us  [shards(): pl.pallas_call(kernel, out_shape=jax.ShapeDtypeStruct((512, 2048), F32),...]
where the time goes in v4:
time: 63.6 us
  Pallas kernels  61 us (96%)
  other arithmetic  2.59 us (4%)
    pallas_call x1, Pallas kernels, shards(): pl.pallas_call(kernel, out_shape=jax.ShapeDtypeStruct((512, 2048), F32),...  61 us
    mul x1, other arithmetic, shards(): return gram * (1.0 / 2048)  2.59 us

profile of v4, /device:TPU:1, one launch (start us, length us, event | category | flops | bytes accessed | tf_op | source)
XLA Modules:
  0.0 63.6 jit_solution(5468856899508135784)
XLA Ops:
  0.0 61.0 %shard_map.37 = f32[512,2048]{1,0:T(8,128)S(1)} custom-call(f32[256,512]{1,0:T(8,128)} %counts.1, f32[1,512]{1,0:T(1,128)} %bitcast.2, f32[1,512]{1,0:T(1,128)} %bitcast.3), custom_call_target="tpu_custom_call" | custom-call | flops 4294967296 | bytes 5242880 | tf_op jit(solution)/shard_map/pallas_call | solution.py:394
  61.0 2.6 %broadcast_multiply_fusion = f32[512,2048]{1,0:T(8,128)} fusion(f32[512,2048]{1,0:T(8,128)S(1)} %shard_map.37), kind=kLoop, calls=%fused_computation | loop fusion | flops 1048576 | bytes 8388608 | tf_op jit(solution)/shard_map/mul | solution.py:431

commit v5 on v4

--- a/solution.py
+++ b/solution.py
@@ -248,7 +248,9 @@
         right = cols[which, j, whose, :, :, first:last].reshape(256, last - first)
         start = pl.multiple_of((whose * 2 + which) * 512 + first, 128)
         columns = pl.ds(start, last - first)
-        out[:, columns] += jnp.dot(lhs[q], right, preferred_element_type=F32)
+        out[:, columns] = (
+            out[:, columns] + jnp.dot(lhs[q], right, preferred_element_type=F32)
+        ) * (1.0 / 2048)
 
     def multiply(s, *qs):
         for q in qs:
@@ -325,6 +327,13 @@
         if q < 7:
             hand(q, 1).wait_send()
 
+    def early_left():
+        ring_left(1)
+        for side in (0, 1):
+            swap(0, 1, side).wait_send()
+        for q in range(5):
+            swaps_left(q)
+
     def last_swapped():
         for side in (0, 1):
             swapped(7, 0, side).wait_recv()
@@ -341,7 +350,7 @@
         (2, 1): [lambda: finish(3), lambda: finish(4), rows_arrive, lambda: prepare(0, 1, 2), lambda: multiply(0, 0, 1, 2)],
         (1, 2): [lambda: multiply(1, 0, 1, 2), lambda: prepare(3, 4)],
         (0, 3): [lambda: multiply(0, 3, 4), lambda: multiply(1, 3, 4), lambda: prepare(5, 6, 7)],
-        (2, 2): [lambda: finish(5), lambda: finish(6), lambda: multiply(0, 5, 6), lambda: ring_left(0), rows_left],
+        (2, 2): [lambda: finish(5), lambda: finish(6), lambda: multiply(0, 5, 6), lambda: ring_left(0), rows_left, early_left],
         (1, 3): [lambda: multiply(1, 5, 6), last_swapped],
     }
     order = (
@@ -379,11 +388,9 @@
     for kind in (0, 1):
         for side in (0, 1):
             last_hand(kind, side).wait_send()
-    for side in (0, 1):
-        swap(0, 1, side).wait_send()
-    for q in range(8):
+    for q in (5, 6, 7):
         swaps_left(q)
-    for hop in (1, 2, 3):
+    for hop in (2, 3):
         ring_left(hop)
 
 
@@ -428,7 +435,25 @@
             flops=2 * 512 * 2048 * 2048, bytes_accessed=5 << 20, transcendentals=1 << 17
         ),
     )(*operands)
-    return gram * (1.0 / 2048)
+
+    def store(src, dst, sems):
+        copies = [
+            pltpu.make_async_copy(src.at[pl.ds(64 * n, 64)], dst.at[pl.ds(64 * n, 64)], sems.at[n])
+            for n in range(8)
+        ]
+        for copy in copies:
+            copy.start()
+        for copy in copies:
+            copy.wait()
+
+    return pl.pallas_call(
+        store,
+        out_shape=jax.ShapeDtypeStruct((512, 2048), F32),
+        in_specs=[pl.BlockSpec(memory_space=pltpu.VMEM)],
+        out_specs=pl.BlockSpec(memory_space=pltpu.HBM),
+        scratch_shapes=[dma((8,))],
+        compiler_params=pltpu.CompilerParams(vmem_limit_bytes=8 << 20),
+    )(gram)
 
 
 def solution(mesh):

time: 63.6 us -> 63.1 us (level)
  other arithmetic: 2.59 us -> 0 us
  Pallas kernels: 61 us -> 63 us
    mul x1 -> x0, other arithmetic: 2.59 us -> none  [shards(): return gram * (1.0 / 2048)]
    pallas_call x0 -> x1, Pallas kernels: none -> 2.07 us  [shards(): pl.pallas_call(store, out_shape=jax.ShapeDtypeStruct((512, 2048), F32), i...]
where the time goes in v5:
time: 63.1 us; the launch traced here: 63 us
  Pallas kernels  63 us (100%)
    pallas_call x1, Pallas kernels, shards(): pl.pallas_call(kernel, out_shape=jax.ShapeDtypeStruct((512, 2048), F32),...  60.9 us
    pallas_call x1, Pallas kernels, shards(): pl.pallas_call(store, out_shape=jax.ShapeDtypeStruct((512, 2048), F32), i...  2.07 us

profile of v5, /device:TPU:1, one launch (start us, length us, event | category | flops | bytes accessed | tf_op | source)
XLA Modules:
  0.0 63.0 jit_solution(10621929534005400035)
XLA Ops:
  0.0 60.9 %shard_map.37.src = f32[512,2048]{1,0:T(8,128)S(1)} custom-call(f32[256,512]{1,0:T(8,128)} %counts.1, f32[1,512]{1,0:T(1,128)} %bitcast.2, f32[1,512]{1,0:T(1,128)} %bitcast.3), custom_call_target="tpu_custom_call" | custom-call | flops 4294967296 | bytes 5242880 | tf_op jit(solution)/shard_map/pallas_call | solution.py:401
  60.9 2.1 %shard_map.38 = f32[512,2048]{1,0:T(8,128)} custom-call(f32[512,2048]{1,0:T(8,128)S(1)} %shard_map.37.src), custom_call_target="tpu_custom_call" | custom-call | tf_op jit(solution)/shard_map/pallas_call | solution.py:449

commit v6 on v5

--- a/solution.py
+++ b/solution.py
@@ -340,6 +340,8 @@
             last_hand(0, side).start()
         product(7, 0, True)
         product(7, 1, True, wide, 512)
+        handed(7, 0).wait_recv()
+        product(7, 0, False)
 
     wide = max(SHARED)
     beside = {
@@ -376,8 +378,6 @@
         for action in beside.get((p, hop), ()):
             action()
     product(7, 1, True, 0, wide)
-    handed(7, 0).wait_recv()
-    product(7, 0, False)
     for side in (0, 1):
         last_handed(0, side).wait_recv()
     product(7, 1, False, wide, 512)

time: 63.1 us -> 63.4 us (level)
  no operation moved by 1% of the time
where the time goes in v6:
time: 63.4 us; the launch traced here: 63.3 us
  Pallas kernels  63.3 us (100%)
    pallas_call x1, Pallas kernels, shards(): pl.pallas_call(kernel, out_shape=jax.ShapeDtypeStruct((512, 2048), F32),...  61.2 us
    pallas_call x1, Pallas kernels, shards(): pl.pallas_call(store, out_shape=jax.ShapeDtypeStruct((512, 2048), F32), i...  2.07 us

profile of v6, /device:TPU:1, one launch (start us, length us, event | category | flops | bytes accessed | tf_op | source)
XLA Modules:
  0.0 63.3 jit_solution(15004830263963508285)
XLA Ops:
  0.0 61.2 %shard_map.37.src = f32[512,2048]{1,0:T(8,128)S(1)} custom-call(f32[256,512]{1,0:T(8,128)} %counts.1, f32[1,512]{1,0:T(1,128)} %bitcast.2, f32[1,512]{1,0:T(1,128)} %bitcast.3), custom_call_target="tpu_custom_call" | custom-call | flops 4294967296 | bytes 5242880 | tf_op jit(solution)/shard_map/pallas_call | solution.py:401
  61.2 2.1 %shard_map.38 = f32[512,2048]{1,0:T(8,128)} custom-call(f32[512,2048]{1,0:T(8,128)S(1)} %shard_map.37.src), custom_call_target="tpu_custom_call" | custom-call | tf_op jit(solution)/shard_map/pallas_call | solution.py:449
